TPU v7x, 32 devices: a whole 2x2x4 slice. The times are simulated.
32 devices in a mesh: groups: 1, expert: 32 (over z, y, x, core).
Axes of the slice: x: 2, y: 2, z: 4, core: 2. Of those that a mesh axis runs over, the one named last changes fastest.
Arguments:
- tokens: bfloat16 [512, 8192], P(('groups', 'expert')), may hold values from -6 to 6
- gate_up: bfloat16 [32, 4096, 512], P(('groups', 'expert')), may hold values from -0.0625 to 0.0625
- down_proj: bfloat16 [32, 256, 4096], P(('groups', 'expert')), may hold values from -0.375 to 0.375
- expert_ids: int32 [512, 8], P(('groups', 'expert')), may hold values from 0 to 15, all different within a row; in each aligned block of 16 rows (0 to 15, 16 to 31, ...) at most 10 rows name the same one
- combine: float32 [512, 8], P(('groups', 'expert')), may hold values from 0.05 to 0.3
- teacher: bfloat16 [512, 8192], P(('groups', 'expert')), may hold values from -4 to 4
Outputs:
- student: bfloat16 [512, 8192], P(('groups', 'expert'))
- down_grad: bfloat16 [32, 256, 4096], P(('groups', 'expert'))
Inputs may be any that keep to these rules, and one draw needn't show every extreme that they name: `expert_ids`: each row names 8 different experts; within the rows of one device no expert is named by more than 10 rows, a bound that some block reaches.
All inputs are finite; a program needn't handle non-finite values.
Results may differ from a plain program's by a relative error of at most 0.0072.
Values may be sent and summed in bfloat16 or wider, within the bound.
A program may use at most 64 MiB of HBM per device.

v0:
```python
import jax
import jax.numpy as jnp
from jax import lax
from jax.sharding import PartitionSpec as P


def from_partner(block, axis, stride):
    count = lax.axis_size(axis)
    route = []
    for low in range(count):
        high = low | 1 << stride
        if high != low and high < count:
            route += [(low, high), (high, low)]
    return lax.ppermute(block, axis, route)


def shards(tokens, gate_up, down_proj, expert_ids, combine, teacher):
    row_count, width = tokens.shape
    top_count = expert_ids.shape[1]
    halves = lax.axis_size("expert")
    experts = halves // 2
    unit_count = down_proj.shape[1]
    half_width = width // 2
    mean_load = row_count * top_count // experts
    capacity = min(row_count, mean_load + max(2, mean_load // 3))
    pair_count = row_count * top_count
    flat_expert = expert_ids.reshape(-1)
    onehot = (flat_expert[:, None] == jnp.arange(experts, dtype=jnp.int32)[None, :]).astype(
        jnp.int32
    )
    before = jnp.cumsum(onehot, axis=0) - onehot
    position = jnp.sum(before * onehot, axis=1)
    slot_index = flat_expert * capacity + position
    slot_pair = jnp.full((experts * capacity,), pair_count, jnp.int32)
    slot_pair = slot_pair.at[slot_index].set(jnp.arange(pair_count, dtype=jnp.int32))
    slot_row = jnp.where(slot_pair < pair_count, slot_pair // top_count, row_count)
    half_side = jnp.arange(2, dtype=jnp.int32)[None, :, None]
    row_pick = (slot_row.reshape(experts, 1, capacity) * 2 + half_side).reshape(-1)
    outbox = jnp.take(
        tokens.reshape(row_count * 2, half_width), row_pick, axis=0, mode="fill", fill_value=0
    )
    outbox = outbox.reshape(halves, capacity, half_width)
    gate_local = gate_up[0]
    down_local = down_proj[0]
    arrived = lax.all_to_all(outbox, "expert", split_axis=0, concat_axis=0, tiled=True)
    slot_total = arrived.shape[1]
    rows_in = arrived.reshape(-1, half_width)
    partial_value = jnp.dot(rows_in, gate_local, preferred_element_type=jnp.float32)
    partner = from_partner(partial_value, "expert", 0)
    summed = partial_value + partner
    hidden = (jax.nn.silu(summed[:, :unit_count]) * summed[:, unit_count:]).astype(jnp.bfloat16)
    result = jnp.dot(hidden, down_local, preferred_element_type=jnp.float32).astype(jnp.bfloat16)
    result, hidden = (
        result.reshape(halves, slot_total, half_width),
        hidden.reshape(halves, slot_total, unit_count),
    )
    returned = lax.all_to_all(result, "expert", split_axis=0, concat_axis=0, tiled=True)
    grouped = returned.reshape(experts, 2, capacity, half_width)
    pair_out = grouped[flat_expert, :, position].reshape(row_count, top_count, width)
    student_sum = jnp.sum(combine[:, :, None] * pair_out.astype(jnp.float32), axis=1)
    student = student_sum.astype(jnp.bfloat16)
    error_rows = student.astype(jnp.float32) - teacher.astype(jnp.float32)
    scaled = (combine[:, :, None] * error_rows[:, None, :]).astype(jnp.bfloat16)
    pair_pick = (slot_pair.reshape(experts, 1, capacity) * 2 + half_side).reshape(-1)
    error_box = jnp.take(
        scaled.reshape(pair_count * 2, half_width), pair_pick, axis=0, mode="fill", fill_value=0
    )
    error_box = error_box.reshape(halves, capacity, half_width)
    error_in = lax.all_to_all(error_box, "expert", split_axis=0, concat_axis=0, tiled=True)
    gradient = jnp.einsum(
        "su,sd->ud",
        hidden.reshape(-1, unit_count),
        error_in.reshape(-1, half_width),
        preferred_element_type=jnp.float32,
    )
    return (student, gradient.astype(jnp.bfloat16).reshape(1, unit_count, half_width))


def solution(mesh):
    in_specs = (
        P(("groups", "expert"), None),
        P(("groups", "expert"), None, None),
        P(("groups", "expert"), None, None),
        P(("groups", "expert"), None),
        P(("groups", "expert"), None),
        P(("groups", "expert"), None),
    )
    out_specs = (P(("groups", "expert"), None), P(("groups", "expert"), None, None))
    return jax.shard_map(shards, mesh=mesh, in_specs=in_specs, out_specs=out_specs, check_vma=False)
```

profile of v0, /device:TPU:0, one launch (start us, length us, event | category | flops | bytes accessed | tf_op | source)
XLA Modules:
  0.0 378.1 jit_solution(419564975656376688)
XLA Ops:
  0.6 0.0 copy-start
  0.6 0.9 copy.16
  1.6 0.1 eq.15
  1.6 0.1 reshape.217
  1.7 0.1 fusion.5
  1.8 0.2 reduce_window_sum.11
  2.0 0.2 select_reduce_fusion
  2.2 1.0 scatter_custom_fusion
  3.2 0.1 mul.67
  3.3 0.1 add.167
  3.5 1.1 reshape.218
  4.5 3.9 %gather_fusion = bf16[320,4096]{1,0:T(8,128)(2,1)} fusion(bf16[32,4096]{1,0:T(8,128)(2,1)S(1)} %reshape.218, s32[1024]{0:T(1024)S(1)} %pad_clamp_fusion.1), kind=kCustom, calls=%fused_computation | custom fusion | bytes 5244160 | tf_op jit(solution)/shard_map/jit(_take)/gather | solution.py:39
  8.4 4.6 %gather.16 = bf16[32,10,4096]{2,1,0:T(8,128)(2,1)} reshape(bf16[320,4096]{1,0:T(8,128)(2,1)} %gather_fusion) | data formatting | bytes 5242880 | tf_op jit(solution)/shard_map/jit(_take)/gather | solution.py:39
  13.0 2.5 broadcast_select_fusion.1
  15.6 100.9 %all_to_all.15 = bf16[32,10,4096]{2,1,0:T(8,128)(2,1)} all-to-all(bf16[32,10,4096]{2,1,0:T(8,128)(2,1)S(1)} %broadcast_select_fusion.1), channel_id=1, replica_groups=mesh['groups'=1,'expert'=32] {'expert'}, dimensions={0} | all-to-all | bytes 5242880 | tf_op jit(solution)/shard_map/all_to_all | solution.py:45
  116.4 4.7 %reshape.219 = bf16[320,4096]{1,0:T(8,128)(2,1)} reshape(bf16[32,10,4096]{2,1,0:T(8,128)(2,1)} %all_to_all.15) | data formatting | bytes 5242880 | tf_op jit(solution)/shard_map/reshape | solution.py:47
  121.1 4.5 %fusion.1 = f32[320,512]{1,0:T(8,128)S(1)} fusion(bf16[320,4096]{1,0:T(8,128)(2,1)} %reshape.219, bf16[1,4096,512]{2,1,0:T(8,128)(2,1)} %param.7), kind=kOutput, calls=%fused_computation.7 | convolution fusion | flops 1342177280 | bytes 7471104 | tf_op jit(solution)/shard_map/dot_general | solution.py:48
  125.6 0.1 collective-permute-start
  125.7 2.1 collective-permute-done
  127.8 0.1 add.170
  127.9 0.1 fusion.4
  128.0 0.0 copy-done
  128.0 2.4 convolution_convert_fusion
  130.4 4.6 %reshape.220 = bf16[32,10,4096]{2,1,0:T(8,128)(2,1)} reshape(bf16[320,4096]{1,0:T(8,128)(2,1)} %convolution_convert_fusion) | data formatting | bytes 5242880 | tf_op jit(solution)/shard_map/reshape | solution.py:54
  135.0 0.0 copy-start.4
  135.0 4.0 %all-to-all-start.1 = ((bf16[32,10,4096]{2,1,0:T(8,128)(2,1)}), bf16[32,10,4096]{2,1,0:T(8,128)(2,1)}, u32[]{:S(2)}, u32[]{:S(2)}) async-start(bf16[32,10,4096]{2,1,0:T(8,128)(2,1)} %reshape.220), calls=%async_computation.1 | async-start | bytes 8388608 | tf_op jit(solution)/shard_map/all_to_all | solution.py:57
  139.0 0.0 copy-done.4
  139.0 0.1 copy.15
  139.1 0.1 mul.72
  139.2 0.1 add.181
  139.4 93.4 %all-to-all-done.1 = bf16[32,10,4096]{2,1,0:T(8,128)(2,1)} async-done(((bf16[32,10,4096]{2,1,0:T(8,128)(2,1)}), bf16[32,10,4096]{2,1,0:T(8,128)(2,1)}, u32[]{:S(2)}, u32[]{:S(2)}) %all-to-all-start.1) | async-done | bytes 2621472 | tf_op jit(solution)/shard_map/all_to_all | solution.py:57
  232.8 6.5 %copy.19 = bf16[16,2,10,4096]{3,1,2,0:T(2,128)(2,1)} copy(bf16[16,2,10,4096]{3,2,1,0:T(8,128)(2,1)} %bitcast.5) | data formatting | bytes 5242880 | tf_op jit(solution)/shard_map/reshape | solution.py:58
  239.3 10.2 %gather_fusion.1 = bf16[128,2,4096]{2,1,0:T(2,128)(2,1)S(1)} fusion(bf16[16,2,10,4096]{3,1,2,0:T(2,128)(2,1)} %copy.19, s32[128]{0:T(128)S(1)} %get-tuple-element.4), kind=kCustom, calls=%fused_computation.1 | custom fusion | bytes 4195328 | tf_op jit(solution)/shard_map/gather | solution.py:59
  249.4 2.9 reshape.224
  252.3 0.0 copy-start.3
  252.3 3.6 multiply_reduce_fusion
  255.9 0.0 copy-done.3
  255.9 0.0 copy-start.2
  255.9 0.1 convert_subtract_fusion
  256.0 1.7 multiply_convert_fusion
  257.7 2.7 convert_element_type.43
  260.4 0.0 copy-done.2
  260.4 3.9 %gather_fusion.2 = bf16[320,4096]{1,0:T(8,128)(2,1)} fusion(bf16[256,4096]{1,0:T(8,128)(2,1)S(1)} %convert_element_type.43, s32[1024]{0:T(1024)S(1)} %pad_clamp_fusion), kind=kCustom, calls=%fused_computation.2 | custom fusion | bytes 5244160 | tf_op jit(solution)/shard_map/jit(_take)/gather | solution.py:65
  264.3 4.6 %gather.19 = bf16[32,10,4096]{2,1,0:T(8,128)(2,1)} reshape(bf16[320,4096]{1,0:T(8,128)(2,1)} %gather_fusion.2) | data formatting | bytes 5242880 | tf_op jit(solution)/shard_map/jit(_take)/gather | solution.py:65
  268.9 2.5 broadcast_select_fusion
  271.5 97.4 %all_to_all.16 = bf16[32,10,4096]{2,1,0:T(8,128)(2,1)} all-to-all(bf16[32,10,4096]{2,1,0:T(8,128)(2,1)S(1)} %broadcast_select_fusion), channel_id=1, replica_groups=mesh['groups'=1,'expert'=32] {'expert'}, dimensions={0} | all-to-all | bytes 5242880 | tf_op jit(solution)/shard_map/all_to_all | solution.py:69
  368.9 0.0 copy-start.1
  368.9 4.8 %reshape.222 = bf16[320,4096]{1,0:T(8,128)(2,1)} reshape(bf16[32,10,4096]{2,1,0:T(8,128)(2,1)} %all_to_all.16) | data formatting | bytes 5242880 | tf_op jit(solution)/shard_map/reshape | solution.py:73
  373.7 4.3 %fusion = bf16[1,256,4096]{2,1,0:T(8,128)(2,1)} fusion(bf16[320,256]{1,0:T(8,128)(2,1)S(1)} %fusion.4, bf16[320,4096]{1,0:T(8,128)(2,1)} %reshape.222), kind=kOutput, calls=%fused_computation.6 | convolution fusion | flops 672137216 | bytes 4882432 | tf_op jit(solution)/shard_map/su,sd->ud/dot_general | solution.py:70
  378.1 0.0 copy-done.1
  (11 shorter events, 0.1 us)
Async XLA Ops:
  0.6 127.4 %copy-start = (bf16[1,256,4096]{2,1,0:T(8,128)(2,1)S(1)}, bf16[1,256,4096]{2,1,0:T(8,128)(2,1)}, u32[]{:S(2)}) copy-start(bf16[1,256,4096]{2,1,0:T(8,128)(2,1)} %param.8) | copy-start | bytes 6291460
  125.6 2.2 collective-permute-start
  135.0 4.0 %copy-start.4 = (f32[16,8]{0,1:T(8,128)S(1)}, f32[16,8]{0,1:T(8,128)}, u32[]{:S(2)}) copy-start(f32[16,8]{0,1:T(8,128)} %param.10) | copy-start | bytes 1540
  135.0 97.8 %all-to-all-start.1 = ((bf16[32,10,4096]{2,1,0:T(8,128)(2,1)}), bf16[32,10,4096]{2,1,0:T(8,128)(2,1)}, u32[]{:S(2)}, u32[]{:S(2)}) async-start(bf16[32,10,4096]{2,1,0:T(8,128)(2,1)} %reshape.220), calls=%async_computation.1 | async-start | bytes 8388608 | tf_op jit(solution)/shard_map/all_to_all | solution.py:57
  252.3 3.6 copy-start.3
  255.9 4.5 %copy-start.2 = (bf16[16,8192]{1,0:T(8,128)(2,1)}, bf16[16,8192]{1,0:T(8,128)(2,1)S(1)}, u32[]{:S(2)}) copy-start(bf16[16,8192]{1,0:T(8,128)(2,1)S(1)} %multiply_reduce_fusion) | copy-start | bytes 786436
  368.9 9.2 %copy-start.1 = (bf16[1,256,4096]{2,1,0:T(8,128)(2,1)S(1)}, bf16[1,256,4096]{2,1,0:T(8,128)(2,1)}, u32[]{:S(2)}) copy-start(bf16[1,256,4096]{2,1,0:T(8,128)(2,1)} %param.8) | copy-start | bytes 6291460
where the time goes:
time: 379 us; the launch traced here: 378 us
  blocking collectives  198 us (52%)
  waiting for transfers between devices  95.5 us (25%)
  local copies, waits for them, and re-layouts  57 us (15%)
  matrix products  11.2 us (3%)
  other arithmetic  11.1 us (3%)
  starting transfers between devices  4.09 us (1%)
    all_to_all x1, blocking collectives, shards(): lax.all_to_all(outbox, 'expert', split_axis=0, concat_axis=0, tiled=True)  101 us
    all_to_all x1, blocking collectives, shards(): lax.all_to_all(error_box, 'expert', split_axis=0, concat_axis=0, tiled=True)  97.4 us
    all_to_all x1, waiting for transfers between devices, shards(): lax.all_to_all(result, 'expert', split_axis=0, concat_axis=0, tiled=True)  93.4 us
    gather x1, local copies, waits for them, and re-layouts, shards(): grouped[flat_expert, :, position].reshape(row_count, top_count, width)  10.2 us
    gather x2, local copies, waits for them, and re-layouts, shards(): jnp.take(scaled.reshape(pair_count * 2, half_width), pair_pick, axis=0, m...  8.49 us
    gather x2, local copies, waits for them, and re-layouts, shards(): jnp.take(tokens.reshape(row_count * 2, half_width), row_pick, axis=0, mod...  8.49 us
  transfers between devices with their start and end apart: 2, of which 2 were waited for; matrix products, arithmetic and copies ran while one was open for 0% of the time, Pallas kernels for 0%

commit v1 on v0

v1 whole, which is shorter than its diff:
```python
import jax
import jax.numpy as jnp
from jax import lax
from jax.sharding import PartitionSpec as P


def swap_cores(block):
    count = lax.axis_size("expert")
    return lax.ppermute(block, "expert", [(i, i ^ 1) for i in range(count)])


def dense_weights(expert_ids, combine, experts):
    match = expert_ids[:, :, None] == jnp.arange(experts, dtype=jnp.int32)[None, None, :]
    return jnp.sum(jnp.where(match, combine[:, :, None], 0.0), axis=1)


def shards(tokens, gate_up, down_proj, expert_ids, combine, teacher):
    row_count, width = tokens.shape
    count = lax.axis_size("expert")
    experts = count // 2
    unit_count = down_proj.shape[1]
    half = width // 2
    me = lax.axis_index("expert")
    expert, core = me // 2, me % 2
    same_core = [list(range(0, count, 2)), list(range(1, count, 2))]

    def chip_rows(rows):
        kept = lax.dynamic_slice(rows, (0, core * half), (row_count, half))
        given = lax.dynamic_slice(rows, (0, (1 - core) * half), (row_count, half))
        got = swap_cores(given)
        first = jnp.where(core == 0, kept, got)
        second = jnp.where(core == 0, got, kept)
        return jnp.concatenate([first, second], axis=0)

    def gather(block):
        return lax.all_gather(block, "expert", axis_index_groups=same_core, axis=0, tiled=True)

    weights = lax.all_gather(dense_weights(expert_ids, combine, experts), "expert", axis=0, tiled=True)
    weight = lax.dynamic_slice(weights, (0, expert), (weights.shape[0], 1))
    taught = chip_rows(teacher)
    rows_in = gather(chip_rows(tokens))
    partial = jnp.dot(rows_in, gate_up[0], preferred_element_type=jnp.float32)
    pre = partial + swap_cores(partial)
    hidden = jax.nn.silu(pre[:, :unit_count]) * pre[:, unit_count:]
    weighed = (weight * hidden).astype(jnp.bfloat16)
    part = jnp.dot(weighed, down_proj[0], preferred_element_type=jnp.float32).astype(jnp.bfloat16)
    block = lax.psum_scatter(part, "expert", axis_index_groups=same_core, scatter_dimension=0, tiled=True)
    error = (block.astype(jnp.float32) - taught.astype(jnp.float32)).astype(jnp.bfloat16)
    mine = lax.dynamic_slice(block, (core * row_count, 0), (row_count, half))
    theirs = swap_cores(lax.dynamic_slice(block, ((1 - core) * row_count, 0), (row_count, half)))
    student = jnp.concatenate(
        [jnp.where(core == 0, mine, theirs), jnp.where(core == 0, theirs, mine)], axis=1
    )
    errors = gather(error)
    gradient = jnp.einsum("su,sd->ud", weighed, errors, preferred_element_type=jnp.float32)
    return (student, gradient.astype(jnp.bfloat16).reshape(1, unit_count, half))


def solution(mesh):
    in_specs = (
        P(("groups", "expert"), None),
        P(("groups", "expert"), None, None),
        P(("groups", "expert"), None, None),
        P(("groups", "expert"), None),
        P(("groups", "expert"), None),
        P(("groups", "expert"), None),
    )
    out_specs = (P(("groups", "expert"), None), P(("groups", "expert"), None, None))
    return jax.shard_map(shards, mesh=mesh, in_specs=in_specs, out_specs=out_specs, check_vma=False)
```

time: 379 us -> 324 us (0.85)
  blocking collectives: 198 us -> 39.9 us
  waiting for transfers between devices: 95.5 us -> 244 us
  local copies, waits for them, and re-layouts: 57 us -> 2.4 us
  between operations: 0.88 us -> 13.9 us
    all_to_all x2 -> x0, blocking collectives: 198 us -> none  [the longest x1 101 us: shards(): lax.all_to_all(outbox, 'expert', split_axis=0, concat_axis=0, tiled=True)]
    all_gather x0 -> x2, waiting for transfers between devices: none -> 152 us  [gather(): lax.all_gather(block, 'expert', axis_index_groups=same_core, axis=0, tile...]
    all_to_all x1 -> x0, waiting for transfers between devices: 93.4 us -> none  [shards(): lax.all_to_all(result, 'expert', split_axis=0, concat_axis=0, tiled=True)]
    reduce_scatter x0 -> x1, waiting for transfers between devices: none -> 88.9 us  [shards(): lax.psum_scatter(part, 'expert', axis_index_groups=same_core, scatter_dim...]
    all_gather x0 -> x1, blocking collectives: none -> 39.9 us  [shards(): lax.all_gather(dense_weights(expert_ids, combine, experts), 'expert', axi...]
    gather x5 -> x0, local copies, waits for them, and re-layouts: 27.2 us -> none  [the longest x1 10.2 us: shards(): grouped[flat_expert, :, position].reshape(row_count, top_count, width)]
    reshape x6 -> x0, local copies, waits for them, and re-layouts: 21.7 us -> none  [the longest x1 6.46 us: shards(): grouped = returned.reshape(experts, 2, capacity, half_width)]
    convert_element_type x2 -> x0, local copies, waits for them, and re-layouts: 5.63 us -> none  [the longest x1 2.89 us: shards(): pair_out.astype(jnp.float32)]
  transfers between devices with their start and end apart: 2 -> 7, of which waited for: 2 -> 6; matrix products, arithmetic and copies ran while one was open for 0% -> 1% of each run, Pallas kernels for 0% -> 0%
where the time goes in v1:
time: 324 us
  waiting for transfers between devices  244 us (75%)
  blocking collectives  39.9 us (12%)
  matrix products  14 us (4%)
  between operations  13.9 us (4%)
  other arithmetic  7.9 us (2%)
    all_gather x2, waiting for transfers between devices, gather(): lax.all_gather(block, 'expert', axis_index_groups=same_core, axis=0, tile...  152 us
    reduce_scatter x1, waiting for transfers between devices, shards(): lax.psum_scatter(part, 'expert', axis_index_groups=same_core, scatter_dim...  88.9 us
    all_gather x1, blocking collectives, shards(): lax.all_gather(dense_weights(expert_ids, combine, experts), 'expert', axi...  39.9 us
  transfers between devices with their start and end apart: 7, of which 6 were waited for; matrix products, arithmetic and copies ran while one was open for 1% of the time, Pallas kernels for 0%

profile of v1, /device:TPU:0, one launch (start us, length us, event | category | flops | bytes accessed | tf_op | source)
XLA Modules:
  0.0 323.6 jit_solution(1861995214484119071)
XLA Ops:
  7.2 0.0 copy-start
  7.2 0.0 all-gather.3.cloned.1.call-start
  7.2 1.1 constant_dynamic-slice_fusion.2
  8.3 0.5 collective-permute-start
  8.8 1.0 collective-permute-done
  9.8 0.9 broadcast_select_fusion.5
  10.8 0.7 pad_maximum_fusion
  11.5 0.0 all-gather.3.cloned.1.call-update
  11.5 0.0 copy-start.3
  11.5 0.0 copy-start.4
  11.5 0.0 reduce-scatter.2.cloned.1.call-start
  11.6 78.8 %all-gather.3.cloned.1.call-done = bf16[512,4096]{1,0:T(8,128)(2,1)} async-done(((bf16[32,4096]{1,0:T(8,128)(2,1)}), bf16[512,4096]{1,0:T(8,128)(2,1)}) %all-gather.3.cloned.1.call-update) | async-done | bytes 4194320 | tf_op jit(solution)/shard_map/all_gather | solution.py:36
  90.4 5.8 %fusion.1 = f32[512,512]{1,0:T(8,128)S(1)} fusion(bf16[512,4096]{1,0:T(8,128)(2,1)} %all-gather.3.cloned.1.call-done, bf16[1,4096,512]{2,1,0:T(8,128)(2,1)} %param.7), kind=kOutput, calls=%fused_computation.3 | convolution fusion | flops 2147483648 | bytes 9437184 | tf_op jit(solution)/shard_map/dot_general | solution.py:42
  96.1 0.0 copy-start.1
  96.2 0.1 collective-permute-start.1
  96.2 0.0 copy-done.3
  96.2 0.1 copy.15
  96.3 0.0 copy-done.4
  96.3 0.1 copy.14
  96.4 0.1 select_reduce_fusion
  96.5 39.9 %all_gather.9 = f32[512,16]{1,0:T(8,128)S(1)} all-gather(f32[16,16]{1,0:T(8,128)S(1)} %select_reduce_fusion), channel_id=1, replica_groups=mesh['groups'=1,'expert'=32] {'expert'}, dimensions={0}, use_global_device_ids=true | all-gather | bytes 33792 | tf_op jit(solution)/shard_map/all_gather | solution.py:38
  136.4 0.2 dynamic-slice_reduce_fusion
  136.6 0.0 copy-done.1
  136.6 0.0 collective-permute-done.1
  136.6 1.8 add.35
  138.4 0.0 copy-done
  138.4 0.0 copy-start.2
  138.4 3.3 %convolution_convert_fusion = bf16[512,4096]{1,0:T(8,128)(2,1)} fusion(bf16[1,256,4096]{2,1,0:T(8,128)(2,1)S(1)} %copy-done, f32[512,512]{1,0:T(8,128)S(1)} %add.35, f32[512]{0:T(512)S(1)} %dynamic-slice_reduce_fusion), kind=kOutput, calls=%fused_computation | convolution fusion | flops 1076756480 | bytes 7342080 | tf_op jit(solution)/shard_map/dot_general | solution.py:46
  141.7 0.0 reduce-scatter.2.cloned.1.call-update
  141.7 0.0 all-gather.5.cloned.1.call-start
  141.8 0.0 copy-done.2
  141.8 0.4 collective-permute-start.3
  142.2 1.0 collective-permute-done.3
  143.2 1.0 broadcast_select_fusion.1
  144.2 88.9 %reduce-scatter.2.cloned.1.call-done = bf16[32,4096]{1,0:T(8,128)(2,1)} async-done(((bf16[512,4096]{1,0:T(8,128)(2,1)}), bf16[32,4096]{1,0:T(8,128)(2,1)}) %reduce-scatter.2.cloned.1.call-update) | async-done | bytes 262160 | tf_op jit(solution)/shard_map/reduce_scatter | solution.py:47
  233.1 1.7 subtract_convert_fusion
  234.8 0.0 all-gather.5.cloned.1.call-update
  234.8 0.9 constant_dynamic-slice_fusion.1
  235.7 0.1 collective-permute-start.2
  235.8 1.3 collective-permute-done.2
  237.1 1.0 broadcast_select_fusion.3
  238.1 0.7 pad_maximum_fusion.1
  238.8 73.3 %all-gather.5.cloned.1.call-done = bf16[512,4096]{1,0:T(8,128)(2,1)} async-done(((bf16[32,4096]{1,0:T(8,128)(2,1)}), bf16[512,4096]{1,0:T(8,128)(2,1)}) %all-gather.5.cloned.1.call-update) | async-done | bytes 4194320 | tf_op jit(solution)/shard_map/all_gather | solution.py:36
  312.1 4.9 %fusion = bf16[1,256,4096]{2,1,0:T(8,128)(2,1)} fusion(bf16[512,4096]{1,0:T(8,128)(2,1)} %all-gather.5.cloned.1.call-done, f32[512,512]{1,0:T(8,128)S(1)} %add.35, f32[512]{0:T(512)S(1)} %dynamic-slice_reduce_fusion), kind=kOutput, calls=%fused_computation.2 | convolution fusion | flops 1075707904 | bytes 7342080 | tf_op jit(solution)/shard_map/su,sd->ud/dot_general | solution.py:55
  (1 shorter events, 0.0 us)
Async XLA Ops:
  7.2 131.2 %copy-start = (bf16[1,256,4096]{2,1,0:T(8,128)(2,1)S(1)}, bf16[1,256,4096]{2,1,0:T(8,128)(2,1)}, u32[]{:S(2)}) copy-start(bf16[1,256,4096]{2,1,0:T(8,128)(2,1)} %param.8) | copy-start | bytes 6291460
  7.2 83.2 %all-gather.3.cloned.1.call-start = ((), (), s32[]{:S(2)}) async-start(), calls=%async_computation.1 | async-start | bytes 4456448 | tf_op jit(solution)/shard_map/all_gather | solution.py:36
  8.3 1.5 collective-permute-start
  11.5 84.7 %copy-start.3 = (f32[16,8]{0,1:T(8,128)S(1)}, f32[16,8]{0,1:T(8,128)}, u32[]{:S(2)}) copy-start(f32[16,8]{0,1:T(8,128)} %param.10) | copy-start | bytes 1540
  11.5 84.8 %copy-start.4 = (s32[16,8]{0,1:T(8,128)S(1)}, s32[16,8]{0,1:T(8,128)}, u32[]{:S(2)}) copy-start(s32[16,8]{0,1:T(8,128)} %param.9) | copy-start | bytes 1540
  11.5 221.5 %reduce-scatter.2.cloned.1.call-start = ((), (), s32[]{:S(2)}) async-start(), calls=%async_computation.2 | async-start | bytes 4456448 | tf_op jit(solution)/shard_map/reduce_scatter | solution.py:47
  96.1 40.5 %copy-start.1 = (f32[512,512]{1,0:T(8,128)}, f32[512,512]{1,0:T(8,128)S(1)}, u32[]{:S(2)}) copy-start(f32[512,512]{1,0:T(8,128)S(1)} %fusion.1) | copy-start | bytes 3145732
  96.2 40.5 %collective-permute-start.1 = (f32[512,512]{1,0:T(8,128)S(1)}, f32[512,512]{1,0:T(8,128)}, u32[]{:S(2)}, u32[]{:S(2)}) collective-permute-start(f32[512,512]{1,0:T(8,128)S(1)} %fusion.1), channel_id=1, source_target_pairs={{0,1},{1,0},{2,3},{3,2},{4,5},{5,4},{6,7},{7,6},{8,9},{9,8},{10,11... | collective-permute-start | bytes 3145736 | tf_op jit(solution)/shard_map/ppermute | solution.py:9
  138.4 3.4 %copy-start.2 = (bf16[16,8192]{1,0:T(8,128)(2,1)S(1)}, bf16[16,8192]{1,0:T(8,128)(2,1)}, u32[]{:S(2)}) copy-start(bf16[16,8192]{1,0:T(8,128)(2,1)} %param.11) | copy-start | bytes 786436
  141.7 170.4 %all-gather.5.cloned.1.call-start = ((), (), s32[]{:S(2)}) async-start(), calls=%async_computation.3 | async-start | bytes 4456448 | tf_op jit(solution)/shard_map/all_gather | solution.py:36
  141.8 1.4 collective-permute-start.3
  235.7 1.4 collective-permute-start.2
Sparse Core Ops, SparseCore 0:
  11.6 78.6 all-gather.2
  141.8 91.1 reduce-scatter.1
  236.4 75.7 all-gather.4

commit v2 on v1

--- a/solution.py
+++ b/solution.py
@@ -1,7 +1,416 @@
+import functools
+
 import jax
 import jax.numpy as jnp
 from jax import lax
+from jax.experimental import pallas as pl
+from jax.experimental.pallas import tpu as pltpu
 from jax.sharding import PartitionSpec as P
+
+MESH = pl.DeviceIdType.MESH
+RING, LINE, TAIL, TILE = 4, 4, 128, 512
+GATHER_ORDER = ((0, 1, 2, 3), (1, 2, 0, 3), (2, 1, 3, 0), (3, 2, 1, 0))
+REDUCE_ORDER = ((2, 3, 1, 0), (2, 3, 0, 1), (1, 0, 3, 2), (1, 0, 2, 3))
+
+
+def kernel(
+    tokens, gate_up, down_proj, ids, combine, teacher, student_out, grad_out,
+    tok, gate, down, taught, own_pre, got_pre, hidden_t, part, part_a, part_b,
+    part_l, part_r, line_up, line_down, student, errors, total, grad, sem,
+):
+    rows = ids.shape[0]
+    block, plane = 2 * rows, RING * 2 * rows
+    half = down.shape[1]
+    unit_count = down.shape[0]
+    experts = RING * LINE
+    me = lax.axis_index("expert")
+    core, chip = me % 2, me // 2
+    z, y, x = chip // 4, (chip // 2) % 2, chip % 2
+    p = y * 2 + (x + y) % 2
+
+    def device(at_z, q):
+        at_y = q // 2
+        at_x = (q % 2 + at_y) % 2
+        return ((at_z * 2 + at_y) * 2 + at_x) * 2 + core
+
+    partner = me + 1 - 2 * core
+    after, before, across = (p + 1) % 4, (p + 3) % 4, (p + 2) % 4
+    right, left = device(z, after), device(z, before)
+    above, below = device((z + 1) % LINE, p), device((z + LINE - 1) % LINE, p)
+    not_top, not_bottom = z < LINE - 1, z > 0
+    power = (1 + 3 * (z % 2)) * (1 + 15 * (z // 2))
+
+    def order(table, k):
+        packed = sum(table[i][k] * LINE**i for i in range(LINE))
+        return (packed // power) % LINE
+
+    names = {}
+
+    def flag(name, at=0):
+        base = names.setdefault(name, len(names))
+        return sem.at[base * LINE + at]
+
+    pending = []
+
+    def always(body):
+        body()
+
+    def send(source, target, name, at, to, condition=None):
+        copy = pltpu.make_async_remote_copy(
+            src_ref=source, dst_ref=target, send_sem=flag(name + "s", at),
+            recv_sem=flag(name + "r", at), device_id={"expert": to}, device_id_type=MESH,
+        )
+        when = always if condition is None else pl.when(condition)
+
+        @when
+        def _():
+            copy.start()
+
+        pending.append((when, copy))
+
+    def arrived(target, name, at=0):
+        pltpu.make_async_remote_copy(
+            src_ref=target, dst_ref=target, send_sem=flag(name + "s", at),
+            recv_sem=flag(name + "r", at), device_id={"expert": partner}, device_id_type=MESH,
+        ).wait_recv()
+
+    def local(source, target, name):
+        copy = pltpu.make_async_copy(source, target, flag(name))
+        copy.start()
+        return copy
+
+    def span(at_z, q):
+        return pl.ds(pl.multiple_of((at_z * RING + q) * block, block), block)
+
+    def part_span(at_z, q, side):
+        return pl.ds(pl.multiple_of((at_z * RING + q) * block + side * rows, rows), rows)
+
+    def plane_span(at_z):
+        return pl.ds(pl.multiple_of(at_z * plane, plane), plane)
+
+    kept = pl.ds(pl.multiple_of(core * half, half), half)
+    given = pl.ds(pl.multiple_of((1 - core) * half, half), half)
+    my_rows = part_span(z, p, core)
+    its_rows = part_span(z, p, 1 - core)
+    front, tail = pl.ds(0, half), pl.ds(half, TAIL)
+    core_rows = pl.ds(pl.multiple_of(core * rows, rows), rows)
+    other_rows = pl.ds(pl.multiple_of((1 - core) * rows, rows), rows)
+
+    tok_load = local(tokens.at[:, kept], tok.at[my_rows, front], "tok")
+    gate_load = local(gate_up.at[0], gate, "gate")
+    down_load = local(down_proj.at[0], down, "down")
+    taught_load = local(teacher.at[:, kept], taught.at[core_rows, :], "taught")
+
+    barrier = pltpu.get_barrier_semaphore()
+    for to in (partner, right, left):
+        pl.semaphore_signal(barrier, inc=1, device_id={"expert": to}, device_id_type=MESH)
+
+    @pl.when(not_top)
+    def _():
+        pl.semaphore_signal(barrier, inc=1, device_id={"expert": above}, device_id_type=MESH)
+
+    @pl.when(not_bottom)
+    def _():
+        pl.semaphore_signal(barrier, inc=1, device_id={"expert": below}, device_id_type=MESH)
+
+    lane = lax.broadcasted_iota(jnp.int32, (rows, TAIL), 1)
+    weight = jnp.zeros((rows, TAIL), jnp.float32)
+    for k in range(ids.shape[1]):
+        weight += jnp.where(ids[:, k : k + 1] == lax.rem(lane, experts), combine[:, k : k + 1], 0.0)
+    high = weight.astype(jnp.bfloat16).astype(jnp.float32)
+    middle = (weight - high).astype(jnp.bfloat16).astype(jnp.float32)
+    low = weight - high - middle
+    coded = jnp.where(lane < experts, high, jnp.where(lane < 2 * experts, middle, low))
+    coded = jnp.where(lane < 3 * experts, coded, 0.0)
+    tok[my_rows, tail] = coded.astype(jnp.bfloat16)
+
+    pl.semaphore_wait(barrier, 3 + (LINE - 1 - z + LINE - 2) // (LINE - 1) + (z + LINE - 2) // (LINE - 1))
+
+    send(tokens.at[:, given], tok.at[my_rows, front], "tokx", 0, partner)
+    send(tok.at[my_rows, tail], tok.at[my_rows, tail], "tailx", 0, partner)
+    send(teacher.at[:, given], taught.at[core_rows, :], "taughtx", 0, partner)
+    tok_load.wait()
+    arrived(tok.at[its_rows, front], "tokx")
+    arrived(tok.at[its_rows, tail], "tailx")
+
+    def start(buffer, tag, k):
+        at_z = order(GATHER_ORDER, k)
+        here = buffer.at[span(at_z, p)]
+        if k > 0:
+            arrived(here, tag + "z", at_z)
+        send(here, here, tag + "z", at_z, above, (at_z <= z) & not_top)
+        copy = pltpu.make_async_remote_copy(
+            src_ref=here, dst_ref=here, send_sem=flag(tag + "d", at_z),
+            recv_sem=flag(tag + "zr", at_z), device_id={"expert": below}, device_id_type=MESH,
+        )
+        when = pl.when((at_z >= z) & not_bottom)
+
+        @when
+        def _():
+            copy.start()
+
+        pending.append((when, copy))
+        send(here, here, tag + "l", at_z, right)
+        send(here, here, tag + "r", at_z, left)
+
+    def forward(buffer, tag, k):
+        at_z = order(GATHER_ORDER, k)
+        arrived(buffer.at[span(at_z, before)], tag + "l", at_z)
+        piece = buffer.at[part_span(at_z, before, 0)]
+        send(piece, piece, tag + "ol", at_z, right)
+        arrived(buffer.at[span(at_z, after)], tag + "r", at_z)
+        piece = buffer.at[part_span(at_z, after, 1)]
+        send(piece, piece, tag + "or", at_z, left)
+
+    def complete(buffer, tag, k):
+        at_z = order(GATHER_ORDER, k)
+        arrived(buffer.at[part_span(at_z, across, 0)], tag + "ol", at_z)
+        arrived(buffer.at[part_span(at_z, across, 1)], tag + "or", at_z)
+
+    def gathered(buffer, tag, visit):
+        start(buffer, tag, 0)
+        start(buffer, tag, 1)
+        forward(buffer, tag, 0)
+        start(buffer, tag, 2)
+        forward(buffer, tag, 1)
+        complete(buffer, tag, 0)
+        visit(0)
+        start(buffer, tag, 3)
+        forward(buffer, tag, 2)
+        complete(buffer, tag, 1)
+        visit(1)
+        forward(buffer, tag, 3)
+        complete(buffer, tag, 2)
+        visit(2)
+        complete(buffer, tag, 3)
+        visit(3)
+
+    def multiply(k):
+        at_z = order(GATHER_ORDER, k)
+        own_pre[k] = jnp.dot(
+            tok[plane_span(at_z), front], gate[...], preferred_element_type=jnp.float32
+        )
+        send(own_pre.at[k], got_pre.at[k], "pre", k, partner)
+
+    def finish(k):
+        at_z = order(GATHER_ORDER, k)
+        arrived(got_pre.at[k], "pre", k)
+        pre = own_pre[k] + got_pre[k]
+        gated, up = pre[:, :unit_count], pre[:, unit_count:]
+        lanes = lax.broadcasted_iota(jnp.int32, (plane, TAIL), 1)
+        mine = (lax.rem(lanes, experts) == chip) & (lanes < 3 * experts)
+        coded = tok[plane_span(at_z), tail].astype(jnp.float32)
+        share = jnp.sum(jnp.where(mine, coded, 0.0), axis=1, keepdims=True)
+        hidden = gated / (1.0 + jnp.exp(-gated)) * up * share
+        hidden_t[at_z] = hidden.T.astype(jnp.bfloat16)
+        lowered = hidden.astype(jnp.bfloat16)
+
+        @pl.loop(0, half // TILE)
+        def _(t):
+            columns = pl.ds(pl.multiple_of(t * TILE, TILE), TILE)
+            part[plane_span(at_z), columns] = jnp.dot(
+                lowered, down[:, columns], preferred_element_type=jnp.float32
+            ).astype(jnp.bfloat16)
+
+    def send_first(k):
+        at_z = order(REDUCE_ORDER, k)
+        send(part.at[part_span(at_z, across, 0)], part_a.at[at_z], "a", at_z, right)
+        send(part.at[part_span(at_z, across, 1)], part_b.at[at_z], "b", at_z, left)
+        send(part.at[part_span(at_z, after, 1)], part_l.at[at_z, 1], "l1", at_z, right)
+        send(part.at[part_span(at_z, before, 0)], part_r.at[at_z, 0], "r0", at_z, left)
+
+    def add_up(target, *terms):
+        @pl.loop(0, half // TILE)
+        def _(t):
+            columns = pl.ds(pl.multiple_of(t * TILE, TILE), TILE)
+            value = terms[0](columns).astype(jnp.float32)
+            for term in terms[1:]:
+                value += term(columns).astype(jnp.float32)
+            target(columns, value)
+
+    def send_second(k):
+        at_z = order(REDUCE_ORDER, k)
+        for name, got, q, side, to in (
+            ("a", part_a, after, 0, right), ("b", part_b, before, 1, left)
+        ):
+            arrived(got.at[at_z], name, at_z)
+            piece = part_span(at_z, q, side)
+
+            def put(columns, value, piece=piece):
+                part[piece, columns] = value.astype(jnp.bfloat16)
+
+            add_up(put, lambda c, piece=piece: part[piece, c], lambda c, got=got: got[at_z, :, c])
+            if side == 0:
+                send(part.at[piece], part_l.at[at_z, 0], "l0", at_z, to)
+            else:
+                send(part.at[piece], part_r.at[at_z, 1], "r1", at_z, to)
+
+    def reduce_line(k):
+        at_z = order(REDUCE_ORDER, k)
+        for side in range(2):
+            arrived(part_l.at[at_z, side], "l%d" % side, at_z)
+            arrived(part_r.at[at_z, side], "r%d" % side, at_z)
+
+        def summed(put, *more):
+            for side in range(2):
+                piece = part_span(at_z, p, side)
+                add_up(
+                    functools.partial(put, side),
+                    lambda c: part[piece, c],
+                    lambda c: part_l[at_z, side, :, c],
+                    lambda c: part_r[at_z, side, :, c],
+                    *[lambda c, ref=ref: ref[at_z, pl.ds(side * rows, rows), c] for ref in more],
+                )
+
+        if k < LINE - 1:
+            def put(side, columns, value):
+                part[part_span(at_z, p, side), columns] = value.astype(jnp.bfloat16)
+        else:
+            def put(side, columns, value):
+                inner = pl.ds(side * rows, rows)
+                rounded = value.astype(jnp.bfloat16)
+                student[inner, columns] = rounded
+                error = rounded.astype(jnp.float32) - taught[inner, columns].astype(jnp.float32)
+                errors[part_span(at_z, p, side), columns] = error.astype(jnp.bfloat16)
+
+        if k < LINE - 1:
+            from_below, from_above = (at_z > z) & not_bottom, (at_z < z) & not_top
+
+            @pl.when(from_below)
+            def _():
+                arrived(line_up.at[at_z], "u", at_z)
+                summed(put, line_up)
+
+            @pl.when(from_above)
+            def _():
+                arrived(line_down.at[at_z], "d", at_z)
+                summed(put, line_down)
+
+            @pl.when(((at_z > z) & (z == 0)) | ((at_z < z) & (z == LINE - 1)))
+            def _():
+                summed(put)
+
+            mine = part.at[span(at_z, p)]
+            send(mine, line_up.at[at_z], "u", at_z, above, at_z > z)
+            send(mine, line_down.at[at_z], "d", at_z, below, at_z < z)
+        else:
+            @pl.when(z == 0)
+            def _():
+                arrived(line_down.at[at_z], "d", at_z)
+                summed(put, line_down)
+
+            @pl.when(z == LINE - 1)
+            def _():
+                arrived(line_up.at[at_z], "u", at_z)
+                summed(put, line_up)
+
+            @pl.when(not_top & not_bottom)
+            def _():
+                arrived(line_up.at[at_z], "u", at_z)
+                arrived(line_down.at[at_z], "d", at_z)
+                summed(put, line_up, line_down)
+
+    def forward_visit(k):
+        if k == 0:
+            gate_load.wait()
+        multiply(k)
+        if k == 1:
+            down_load.wait()
+        if k in (1, 2):
+            finish(k - 1)
+        if k in (2, 3):
+            finish(k)
+        if k == 2:
+            send_first(0)
+
+    gathered(tok, "t", forward_visit)
+    send_first(1)
+    send_second(0)
+    send_first(2)
+    send_second(1)
+    reduce_line(0)
+    send_first(3)
+    send_second(2)
+    reduce_line(1)
+    send_second(3)
+    reduce_line(2)
+    taught_load.wait()
+    arrived(taught.at[other_rows, :], "taughtx")
+    reduce_line(3)
+
+    stores = [local(student.at[core_rows, :], student_out.at[:, kept], "student")]
+
+    def backward_visit(k):
+        at_z = order(GATHER_ORDER, k)
+        if k == 0:
+            send(student.at[other_rows, :], student_out.at[:, kept], "studentx", 0, partner)
+
+        @pl.loop(0, half // TILE)
+        def _(t):
+            columns = pl.ds(pl.multiple_of(t * TILE, TILE), TILE)
+            value = jnp.dot(
+                hidden_t[at_z], errors[plane_span(at_z), columns], preferred_element_type=jnp.float32
+            )
+            if k > 0:
+                value += total[:, columns]
+            if k < LINE - 1:
+                total[:, columns] = value
+            else:
+                grad[:, columns] = value.astype(jnp.bfloat16)
+
+    gathered(errors, "e", backward_visit)
+    stores.append(local(grad, grad_out.at[0], "grad"))
+    for copy in stores:
+        copy.wait()
+    arrived(student_out.at[:, given], "studentx")
+    for when, copy in pending:
+        @when
+        def _(copy=copy):
+            copy.wait_send()
+
+
+def fused(tokens, gate_up, down_proj, expert_ids, combine, teacher):
+    rows, width = tokens.shape
+    half = width // 2
+    unit_count = down_proj.shape[1]
+    all_rows, block = RING * LINE * 2 * rows, 2 * rows
+    plane = RING * block
+    anywhere, vmem = pl.BlockSpec(memory_space=pl.ANY), pl.BlockSpec(memory_space=pltpu.VMEM)
+    low, full = jnp.bfloat16, jnp.float32
+    return pl.pallas_call(
+        kernel,
+        out_shape=(
+            jax.ShapeDtypeStruct((rows, width), low),
+            jax.ShapeDtypeStruct((1, unit_count, half), low),
+        ),
+        in_specs=[anywhere, anywhere, anywhere, vmem, vmem, anywhere],
+        out_specs=(anywhere, anywhere),
+        scratch_shapes=[
+            pltpu.VMEM((all_rows, half + TAIL), low),
+            pltpu.VMEM((half, 2 * unit_count), low),
+            pltpu.VMEM((unit_count, half), low),
+            pltpu.VMEM((block, half), low),
+            pltpu.VMEM((LINE, plane, 2 * unit_count), full),
+            pltpu.VMEM((LINE, plane, 2 * unit_count), full),
+            pltpu.VMEM((LINE, unit_count, plane), low),
+            pltpu.VMEM((all_rows, half), low),
+            pltpu.VMEM((LINE, rows, half), low),
+            pltpu.VMEM((LINE, rows, half), low),
+            pltpu.VMEM((LINE, 2, rows, half), low),
+            pltpu.VMEM((LINE, 2, rows, half), low),
+            pltpu.VMEM((LINE, block, half), low),
+            pltpu.VMEM((LINE, block, half), low),
+            pltpu.VMEM((block, half), low),
+            pltpu.VMEM((all_rows, half), low),
+            pltpu.VMEM((unit_count, half), full),
+            pltpu.VMEM((unit_count, half), low),
+            pltpu.SemaphoreType.DMA((64 * LINE,)),
+        ],
+        compiler_params=pltpu.CompilerParams(
+            collective_id=0, has_side_effects=True, vmem_limit_bytes=56 * 2**20
+        ),
+        cost_estimate=pl.CostEstimate(flops=5 * 10**9, bytes_accessed=10**7, transcendentals=10**5),
+    )(tokens, gate_up, down_proj, expert_ids, combine, teacher)
 
 
 def swap_cores(block):
@@ -14,7 +423,7 @@
     return jnp.sum(jnp.where(match, combine[:, :, None], 0.0), axis=1)
 
 
-def shards(tokens, gate_up, down_proj, expert_ids, combine, teacher):
+def spread(tokens, gate_up, down_proj, expert_ids, combine, teacher):
     row_count, width = tokens.shape
     count = lax.axis_size("expert")
     experts = count // 2
@@ -66,4 +475,6 @@
         P(("groups", "expert"), None),
     )
     out_specs = (P(("groups", "expert"), None), P(("groups", "expert"), None, None))
+    small = mesh.shape["expert"] == 2 * RING * LINE
+    shards = fused if small else spread
     return jax.shard_map(shards, mesh=mesh, in_specs=in_specs, out_specs=out_specs, check_vma=False)

time: 324 us -> 140 us (0.43)
  waiting for transfers between devices: 244 us -> 0 us
  Pallas kernels: 0 us -> 132 us
  blocking collectives: 39.9 us -> 0 us
  matrix products: 14 us -> 0 us
  between operations: 13.9 us -> 0.64 us
  other arithmetic: 7.9 us -> 0 us
  local copies, waits for them, and re-layouts: 2.4 us -> 7.51 us
    all_gather x2 -> x0, waiting for transfers between devices: 152 us -> none  [gather(): lax.all_gather(block, 'expert', axis_index_groups=same_core, axis=0, tile...]
    pallas_call x0 -> x1, Pallas kernels: none -> 132 us  [fused(): pl.pallas_call(kernel, out_shape=(jax.ShapeDtypeStruct((rows, width), low...]
    reduce_scatter x1 -> x0, waiting for transfers between devices: 88.9 us -> none  [shards(): lax.psum_scatter(part, 'expert', axis_index_groups=same_core, scatter_dim...]
    all_gather x1 -> x0, blocking collectives: 39.9 us -> none  [shards(): lax.all_gather(dense_weights(expert_ids, combine, experts), 'expert', axi...]
    dot_general x3 -> x0, matrix products: 14 us -> none  [the longest x1 5.79 us: shards(): partial = jnp.dot(rows_in, gate_up[0], preferred_element_type=jnp.float32)]
    unnamed x12 -> x4, local copies, waits for them, and re-layouts: 0.18 us -> 7.51 us
    ppermute x4 -> x0, waiting for transfers between devices: 3.32 us -> none  [swap_cores(): return lax.ppermute(block, 'expert', [(i, i ^ 1) for i in range(count)])]
  transfers between devices with their start and end apart: 7 -> 0, of which waited for: 6 -> 0; matrix products, arithmetic and copies ran while one was open for 1% -> 0% of each run, Pallas kernels for 0% -> 0%
where the time goes in v2:
time: 140 us
  Pallas kernels  132 us (94%)
  local copies, waits for them, and re-layouts  7.51 us (5%)
    pallas_call x1, Pallas kernels, fused(): pl.pallas_call(kernel, out_shape=(jax.ShapeDtypeStruct((rows, width), low...  132 us
    unnamed x4, local copies, waits for them, and re-layouts  7.51 us

profile of v2, /device:TPU:0, one launch (start us, length us, event | category | flops | bytes accessed | tf_op | source)
XLA Modules:
  0.0 140.0 jit_solution(5550297114996686344)
XLA Ops:
  0.6 1.4 copy.8.ids
  2.0 1.4 copy.9.combine
  3.3 131.8 %shard_map.77 = (bf16[16,8192]{1,0:T(8,128)(2,1)}, bf16[1,256,4096]{2,1,0:T(8,128)(2,1)}) custom-call(bf16[16,8192]{1,0:T(8,128)(2,1)} %tokens.1, bf16[1,4096,512]{2,1,0:T(8,128)(2,1)} %gate_up.1, bf16[1,256,4096]{2,1,0:T(8,128)(2,1)} %down_proj.1, s32[16,8]{1,0:T(8,128)} %copy.8.ids, f32[16,8]{1,0:T(8,128)} %copy.9.combine, bf16[16,8192]{1,0:T(8,128)(2,1)} %teacher.1), custom_call_target="tpu_custom_call" | custom-call | flops 5000000000 | bytes 10000000 | tf_op jit(solution)/shard_map/pallas_call | solution.py:380
  135.2 1.7 %copy.12 = bf16[16,8192]{1,0:T(8,128)(2,1)} copy(bf16[16,8192]{1,0:T(8,128)(2,1)} %get-tuple-element.4) | data formatting | bytes 524288
  136.8 3.1 %copy.13 = bf16[1,256,4096]{2,1,0:T(8,128)(2,1)} copy(bf16[1,256,4096]{2,1,0:T(8,128)(2,1)} %get-tuple-element.5) | data formatting | bytes 4194304

commit v3 on v2

--- a/solution.py
+++ b/solution.py
@@ -18,7 +18,7 @@
     tok, gate, down, taught, own_pre, got_pre, hidden_t, part, part_a, part_b,
     part_l, part_r, line_up, line_down, student, errors, total, grad, sem,
 ):
-    rows = ids.shape[0]
+    rows = tokens.shape[0]
     block, plane = 2 * rows, RING * 2 * rows
     half = down.shape[1]
     unit_count = down.shape[0]
@@ -48,7 +48,7 @@
 
     def flag(name, at=0):
         base = names.setdefault(name, len(names))
-        return sem.at[base * LINE + at]
+        return sem.at[base * 2 * LINE + at]
 
     pending = []
 
@@ -115,8 +115,10 @@
 
     lane = lax.broadcasted_iota(jnp.int32, (rows, TAIL), 1)
     weight = jnp.zeros((rows, TAIL), jnp.float32)
-    for k in range(ids.shape[1]):
-        weight += jnp.where(ids[:, k : k + 1] == lax.rem(lane, experts), combine[:, k : k + 1], 0.0)
+    named, shares = ids[...].T, combine[...].T
+    for k in range(ids.shape[0]):
+        match = named[:, k : k + 1] == lax.rem(lane, experts)
+        weight += jnp.where(match, shares[:, k : k + 1], 0.0)
     high = weight.astype(jnp.bfloat16).astype(jnp.float32)
     middle = (weight - high).astype(jnp.bfloat16).astype(jnp.float32)
     low = weight - high - middle
@@ -129,41 +131,48 @@
     send(tokens.at[:, given], tok.at[my_rows, front], "tokx", 0, partner)
     send(tok.at[my_rows, tail], tok.at[my_rows, tail], "tailx", 0, partner)
     send(teacher.at[:, given], taught.at[core_rows, :], "taughtx", 0, partner)
-    tok_load.wait()
-    arrived(tok.at[its_rows, front], "tokx")
-    arrived(tok.at[its_rows, tail], "tailx")
 
     def start(buffer, tag, k):
         at_z = order(GATHER_ORDER, k)
-        here = buffer.at[span(at_z, p)]
-        if k > 0:
-            arrived(here, tag + "z", at_z)
-        send(here, here, tag + "z", at_z, above, (at_z <= z) & not_top)
-        copy = pltpu.make_async_remote_copy(
-            src_ref=here, dst_ref=here, send_sem=flag(tag + "d", at_z),
-            recv_sem=flag(tag + "zr", at_z), device_id={"expert": below}, device_id_type=MESH,
-        )
-        when = pl.when((at_z >= z) & not_bottom)
-
-        @when
-        def _():
-            copy.start()
-
-        pending.append((when, copy))
-        send(here, here, tag + "l", at_z, right)
-        send(here, here, tag + "r", at_z, left)
+        first = tag == "t" and k == 0
+        for turn, side in enumerate((core, 1 - core) if first else (0, 1)):
+            at = at_z * 2 + side
+            here = buffer.at[part_span(at_z, p, side)]
+            if k > 0:
+                arrived(here, tag + "z", at)
+            elif first and turn == 0:
+                tok_load.wait()
+            elif first:
+                arrived(tok.at[its_rows, front], "tokx")
+                arrived(tok.at[its_rows, tail], "tailx")
+            send(here, here, tag + "z", at, above, (at_z <= z) & not_top)
+            copy = pltpu.make_async_remote_copy(
+                src_ref=here, dst_ref=here, send_sem=flag(tag + "d", at),
+                recv_sem=flag(tag + "zr", at), device_id={"expert": below}, device_id_type=MESH,
+            )
+            when = pl.when((at_z >= z) & not_bottom)
+
+            @when
+            def _(copy=copy):
+                copy.start()
+
+            pending.append((when, copy))
+            send(here, here, tag + "l", at, right)
+            send(here, here, tag + "r", at, left)
 
     def forward(buffer, tag, k):
         at_z = order(GATHER_ORDER, k)
-        arrived(buffer.at[span(at_z, before)], tag + "l", at_z)
         piece = buffer.at[part_span(at_z, before, 0)]
+        arrived(piece, tag + "l", at_z * 2)
         send(piece, piece, tag + "ol", at_z, right)
-        arrived(buffer.at[span(at_z, after)], tag + "r", at_z)
         piece = buffer.at[part_span(at_z, after, 1)]
+        arrived(piece, tag + "r", at_z * 2 + 1)
         send(piece, piece, tag + "or", at_z, left)
 
     def complete(buffer, tag, k):
         at_z = order(GATHER_ORDER, k)
+        arrived(buffer.at[part_span(at_z, before, 1)], tag + "l", at_z * 2 + 1)
+        arrived(buffer.at[part_span(at_z, after, 0)], tag + "r", at_z * 2)
         arrived(buffer.at[part_span(at_z, across, 0)], tag + "ol", at_z)
         arrived(buffer.at[part_span(at_z, across, 1)], tag + "or", at_z)
 
@@ -220,7 +229,7 @@
         send(part.at[part_span(at_z, before, 0)], part_r.at[at_z, 0], "r0", at_z, left)
 
     def add_up(target, *terms):
-        @pl.loop(0, half // TILE)
+        @pl.loop(0, half // TILE, unroll=4)
         def _(t):
             columns = pl.ds(pl.multiple_of(t * TILE, TILE), TILE)
             value = terms[0](columns).astype(jnp.float32)
@@ -246,69 +255,53 @@
                 send(part.at[piece], part_r.at[at_z, 1], "r1", at_z, to)
 
     def reduce_line(k):
+        for side in range(2):
+            reduce_side(k, side)
+
+    def reduce_side(k, side):
         at_z = order(REDUCE_ORDER, k)
-        for side in range(2):
-            arrived(part_l.at[at_z, side], "l%d" % side, at_z)
-            arrived(part_r.at[at_z, side], "r%d" % side, at_z)
-
-        def summed(put, *more):
-            for side in range(2):
-                piece = part_span(at_z, p, side)
-                add_up(
-                    functools.partial(put, side),
-                    lambda c: part[piece, c],
-                    lambda c: part_l[at_z, side, :, c],
-                    lambda c: part_r[at_z, side, :, c],
-                    *[lambda c, ref=ref: ref[at_z, pl.ds(side * rows, rows), c] for ref in more],
-                )
-
-        if k < LINE - 1:
-            def put(side, columns, value):
-                part[part_span(at_z, p, side), columns] = value.astype(jnp.bfloat16)
-        else:
-            def put(side, columns, value):
-                inner = pl.ds(side * rows, rows)
-                rounded = value.astype(jnp.bfloat16)
+        piece = part_span(at_z, p, side)
+        inner = pl.ds(side * rows, rows)
+        at = at_z * 2 + side
+        arrived(part_l.at[at_z, side], "l%d" % side, at_z)
+        arrived(part_r.at[at_z, side], "r%d" % side, at_z)
+
+        def put(columns, value):
+            rounded = value.astype(jnp.bfloat16)
+            if k < LINE - 1:
+                part[piece, columns] = rounded
+            else:
                 student[inner, columns] = rounded
                 error = rounded.astype(jnp.float32) - taught[inner, columns].astype(jnp.float32)
-                errors[part_span(at_z, p, side), columns] = error.astype(jnp.bfloat16)
+                errors[piece, columns] = error.astype(jnp.bfloat16)
+
+        def summed(up, down_too):
+            more = []
+            if up:
+                arrived(line_up.at[at_z, side], "u", at)
+                more.append(lambda c: line_up[at_z, side, :, c])
+            if down_too:
+                arrived(line_down.at[at_z, side], "d", at)
+                more.append(lambda c: line_down[at_z, side, :, c])
+            add_up(
+                put,
+                lambda c: part[piece, c],
+                lambda c: part_l[at_z, side, :, c],
+                lambda c: part_r[at_z, side, :, c],
+                *more,
+            )
 
         if k < LINE - 1:
-            from_below, from_above = (at_z > z) & not_bottom, (at_z < z) & not_top
-
-            @pl.when(from_below)
-            def _():
-                arrived(line_up.at[at_z], "u", at_z)
-                summed(put, line_up)
-
-            @pl.when(from_above)
-            def _():
-                arrived(line_down.at[at_z], "d", at_z)
-                summed(put, line_down)
-
-            @pl.when(((at_z > z) & (z == 0)) | ((at_z < z) & (z == LINE - 1)))
-            def _():
-                summed(put)
-
-            mine = part.at[span(at_z, p)]
-            send(mine, line_up.at[at_z], "u", at_z, above, at_z > z)
-            send(mine, line_down.at[at_z], "d", at_z, below, at_z < z)
+            pl.when((at_z > z) & not_bottom)(lambda: summed(True, False))
+            pl.when((at_z < z) & not_top)(lambda: summed(False, True))
+            outer = ((at_z > z) & (z == 0)) | ((at_z < z) & (z == LINE - 1))
+            pl.when(outer)(lambda: summed(False, False))
+            send(part.at[piece], line_up.at[at_z, side], "u", at, above, at_z > z)
+            send(part.at[piece], line_down.at[at_z, side], "d", at, below, at_z < z)
         else:
-            @pl.when(z == 0)
-            def _():
-                arrived(line_down.at[at_z], "d", at_z)
-                summed(put, line_down)
-
-            @pl.when(z == LINE - 1)
-            def _():
-                arrived(line_up.at[at_z], "u", at_z)
-                summed(put, line_up)
-
-            @pl.when(not_top & not_bottom)
-            def _():
-                arrived(line_up.at[at_z], "u", at_z)
-                arrived(line_down.at[at_z], "d", at_z)
-                summed(put, line_up, line_down)
+            pl.when(z == 0)(lambda: summed(False, True))
+            pl.when(z == LINE - 1)(lambda: summed(True, False))
+            pl.when(not_top & not_bottom)(lambda: summed(True, True))
 
     def forward_visit(k):
         if k == 0:
@@ -328,8 +321,8 @@
     send_second(0)
     send_first(2)
     send_second(1)
+    send_first(3)
     reduce_line(0)
-    send_first(3)
     send_second(2)
     reduce_line(1)
     send_second(3)
@@ -398,19 +391,19 @@
             pltpu.VMEM((LINE, rows, half), low),
             pltpu.VMEM((LINE, 2, rows, half), low),
             pltpu.VMEM((LINE, 2, rows, half), low),
-            pltpu.VMEM((LINE, block, half), low),
-            pltpu.VMEM((LINE, block, half), low),
+            pltpu.VMEM((LINE, 2, rows, half), low),
+            pltpu.VMEM((LINE, 2, rows, half), low),
             pltpu.VMEM((block, half), low),
             pltpu.VMEM((all_rows, half), low),
             pltpu.VMEM((unit_count, half), full),
             pltpu.VMEM((unit_count, half), low),
-            pltpu.SemaphoreType.DMA((64 * LINE,)),
+            pltpu.SemaphoreType.DMA((120 * LINE,)),
         ],
         compiler_params=pltpu.CompilerParams(
             collective_id=0, has_side_effects=True, vmem_limit_bytes=56 * 2**20
         ),
         cost_estimate=pl.CostEstimate(flops=5 * 10**9, bytes_accessed=10**7, transcendentals=10**5),
-    )(tokens, gate_up, down_proj, expert_ids, combine, teacher)
+    )(tokens, gate_up, down_proj, expert_ids.T, combine.T, teacher)
 
 
 def swap_cores(block):

time: 140 us -> 133 us (0.950)
  Pallas kernels: 132 us -> 127 us
  local copies, waits for them, and re-layouts: 7.51 us -> 4.8 us
    pallas_call x1, Pallas kernels: 132 us -> 127 us  [fused(): pl.pallas_call(kernel, out_shape=(jax.ShapeDtypeStruct((rows, width), low...]
    unnamed x4 -> x2, local copies, waits for them, and re-layouts: 7.51 us -> 4.8 us
where the time goes in v3:
time: 133 us
  Pallas kernels  127 us (95%)
  local copies, waits for them, and re-layouts  4.8 us (4%)
    pallas_call x1, Pallas kernels, fused(): pl.pallas_call(kernel, out_shape=(jax.ShapeDtypeStruct((rows, width), low...  127 us
    unnamed x2, local copies, waits for them, and re-layouts  4.8 us

profile of v3, /device:TPU:0, one launch (start us, length us, event | category | flops | bytes accessed | tf_op | source)
XLA Modules:
  0.0 132.9 jit_solution(1436247478758794225)
XLA Ops:
  0.6 127.5 %shard_map.77 = (bf16[16,8192]{1,0:T(8,128)(2,1)}, bf16[1,256,4096]{2,1,0:T(8,128)(2,1)}) custom-call(bf16[16,8192]{1,0:T(8,128)(2,1)} %tokens.1, bf16[1,4096,512]{2,1,0:T(8,128)(2,1)} %gate_up.1, bf16[1,256,4096]{2,1,0:T(8,128)(2,1)} %down_proj.1, s32[8,16]{1,0:T(8,128)} %bitcast.2, f32[8,16]{1,0:T(8,128)} %bitcast.3, bf16[16,8192]{1,0:T(8,128)(2,1)} %teacher.1), custom_call_target="tpu_custom_call" | custom-call | flops 5000000000 | bytes 10000000 | tf_op jit(solution)/shard_map/pallas_call | solution.py:373
  128.1 1.7 %copy.10 = bf16[16,8192]{1,0:T(8,128)(2,1)} copy(bf16[16,8192]{1,0:T(8,128)(2,1)} %get-tuple-element.4) | data formatting | bytes 524288
  129.8 3.1 %copy.11 = bf16[1,256,4096]{2,1,0:T(8,128)(2,1)} copy(bf16[1,256,4096]{2,1,0:T(8,128)(2,1)} %get-tuple-element.5) | data formatting | bytes 4194304

commit v4 on v3

--- a/solution.py
+++ b/solution.py
@@ -182,10 +182,10 @@
         forward(buffer, tag, 0)
         start(buffer, tag, 2)
         forward(buffer, tag, 1)
+        start(buffer, tag, 3)
+        forward(buffer, tag, 2)
         complete(buffer, tag, 0)
         visit(0)
-        start(buffer, tag, 3)
-        forward(buffer, tag, 2)
         complete(buffer, tag, 1)
         visit(1)
         forward(buffer, tag, 3)
@@ -350,9 +350,12 @@
                 total[:, columns] = value
             else:
                 grad[:, columns] = value.astype(jnp.bfloat16)
+                pltpu.make_async_copy(
+                    grad.at[:, columns], grad_out.at[0, :, columns], flag("grad")
+                ).start()
 
     gathered(errors, "e", backward_visit)
-    stores.append(local(grad, grad_out.at[0], "grad"))
+    stores.append(pltpu.make_async_copy(grad, grad_out.at[0], flag("grad")))
     for copy in stores:
         copy.wait()
     arrived(student_out.at[:, given], "studentx")

time: 133 us -> 132 us (level)
  no operation moved by 1% of the time
where the time goes in v4:
time: 132 us
  Pallas kernels  127 us (96%)
  local copies, waits for them, and re-layouts  4.8 us (4%)
    pallas_call x1, Pallas kernels, fused(): pl.pallas_call(kernel, out_shape=(jax.ShapeDtypeStruct((rows, width), low...  127 us
    unnamed x2, local copies, waits for them, and re-layouts  4.8 us

profile of v4, /device:TPU:0, one launch (start us, length us, event | category | flops | bytes accessed | tf_op | source)
XLA Modules:
  0.0 132.2 jit_solution(7092321280936063200)
XLA Ops:
  0.6 126.8 %shard_map.77 = (bf16[16,8192]{1,0:T(8,128)(2,1)}, bf16[1,256,4096]{2,1,0:T(8,128)(2,1)}) custom-call(bf16[16,8192]{1,0:T(8,128)(2,1)} %tokens.1, bf16[1,4096,512]{2,1,0:T(8,128)(2,1)} %gate_up.1, bf16[1,256,4096]{2,1,0:T(8,128)(2,1)} %down_proj.1, s32[8,16]{1,0:T(8,128)} %bitcast.2, f32[8,16]{1,0:T(8,128)} %bitcast.3, bf16[16,8192]{1,0:T(8,128)(2,1)} %teacher.1), custom_call_target="tpu_custom_call" | custom-call | flops 5000000000 | bytes 10000000 | tf_op jit(solution)/shard_map/pallas_call | solution.py:376
  127.4 1.7 %copy.10 = bf16[16,8192]{1,0:T(8,128)(2,1)} copy(bf16[16,8192]{1,0:T(8,128)(2,1)} %get-tuple-element.4) | data formatting | bytes 524288
  129.1 3.1 %copy.11 = bf16[1,256,4096]{2,1,0:T(8,128)(2,1)} copy(bf16[1,256,4096]{2,1,0:T(8,128)(2,1)} %get-tuple-element.5) | data formatting | bytes 4194304
